TPU v7x, 128 devices: a whole 4x4x4 slice. The times are simulated.
128 devices in a mesh: batch: 8 (over z, core), table: 16 (over y, x).
Axes of the slice: x: 4, y: 4, z: 4, core: 2. Of those that a mesh axis runs over, the one named last changes fastest.
Arguments:
- item_rows: int32 [1024, 64, 3], P(('batch', 'table')), may hold values from 0 to 16383, as said below
- send_order: int32 [1024], P(('batch', 'table')), may hold values from 0 to 7, as said below
- user_lengths: int32 [1024], P(('batch', 'table')), may hold values from 1 to 64, as said below
- tables: bfloat16 [3, 16384, 1024], P(None, 'table'), may hold values from -3 to 3
- w_in: bfloat16 [1, 1024, 4096], replicated, may hold values from -0.1875 to 0.1875
- w_out: bfloat16 [1, 1024, 1024], replicated, may hold values from -0.1875 to 0.1875
- out_grad: bfloat16 [1024, 64, 1024], P(('batch', 'table')), may hold values from -6 to 6
Outputs:
- encoded: bfloat16 [1024, 64, 1024], P(('batch', 'table'))
- table_grad: float32 [3, 16384, 1024], P(None, 'table', 'batch')
Inputs may be any that keep to these rules, and one draw needn't show every extreme that they name: `item_rows`: every id lies in one table's rows. For each user, the 192 ids name rows of each block of 1024 rows exactly 12 times; padded slots carry ids too. `send_order`: each block of 8 entries is a permutation of 0 to 7. `user_lengths`: the first user of every block of 8 has length 64.
All inputs are finite; a program needn't handle non-finite values.
Results may differ from a plain program's by a relative error of at most 0.013.
Values may be sent and summed in bfloat16 or wider, within the bound.
No kernel may reach another device: no remote copies, remote signals or barrier semaphores. Data moves between devices by JAX's collectives and lax.ppermute only.
A program may use at most 192 MiB of HBM per device.

v0:
```python
import jax
import jax.numpy as jnp
from jax import lax
from jax.sharding import PartitionSpec as P

HEADS = 8


epsilon = 1e-05


def normalize_rows(stream):
    center_mean = jnp.mean(stream, axis=-1, keepdims=True)
    centered = stream - center_mean
    variance = jnp.mean(centered * centered, axis=-1, keepdims=True)
    return centered * lax.rsqrt(variance + epsilon)


def hstu_block(stream, w_in_layer, w_out_layer, attend_mask):
    user_count, seq_length, model_width = stream.shape
    head_size = model_width // HEADS
    normed = (
        normalize_rows(stream).astype(jnp.bfloat16).reshape(user_count * seq_length, model_width)
    )
    projected = jax.nn.silu(jnp.dot(normed, w_in_layer, preferred_element_type=jnp.float32))
    projected = projected.reshape(user_count, seq_length, 4, model_width)
    gate_part = projected[:, :, 0]
    value_part = (
        projected[:, :, 1].astype(jnp.bfloat16).reshape(user_count, seq_length, HEADS, head_size)
    )
    query_part = (
        projected[:, :, 2].astype(jnp.bfloat16).reshape(user_count, seq_length, HEADS, head_size)
    )
    key_part = (
        projected[:, :, 3].astype(jnp.bfloat16).reshape(user_count, seq_length, HEADS, head_size)
    )
    scores = jnp.einsum(
        "uqhe,ukhe->uhqk", query_part.astype(jnp.float32), key_part.astype(jnp.float32)
    )
    scores = scores * head_size ** (-0.5)
    weights = (jax.nn.silu(scores) * attend_mask).astype(jnp.bfloat16)
    mixed = jnp.einsum(
        "uhqk,ukhe->uqhe", weights.astype(jnp.float32), value_part.astype(jnp.float32)
    )
    mixed = mixed.reshape(user_count, seq_length, model_width)
    gated = (
        (normalize_rows(mixed) * gate_part)
        .astype(jnp.bfloat16)
        .reshape(user_count * seq_length, model_width)
    )
    update = jnp.dot(gated, w_out_layer, preferred_element_type=jnp.float32)
    return stream + update.reshape(user_count, seq_length, model_width)


def stack_forward(stream, w_in, w_out, attend_mask, live_slots):
    stream = hstu_block(stream, w_in[0], w_out[0], attend_mask)
    return stream * live_slots[:, :, None]


def run_layers(embedded, lengths, cotangent, w_in, w_out):
    seq_length = embedded.shape[1]
    positions = jnp.arange(seq_length, dtype=jnp.int32)
    live_bool = positions[None, :] < lengths[:, None]
    live_slots = live_bool.astype(jnp.float32)
    causal = positions[None, :] <= positions[:, None]
    attend_mask = (causal[None, None, :, :] & live_bool[:, None, :, None]).astype(jnp.float32)

    def forward(stream):
        return stack_forward(stream, w_in, w_out, attend_mask, live_slots)

    output, pullback = jax.vjp(forward, embedded.astype(jnp.float32))
    token_grad = pullback(cotangent.astype(jnp.float32))[0]
    return (output.astype(jnp.bfloat16), token_grad)


def body(item_rows, send_order, user_lengths, tables, w_in, w_out, out_grad):
    batch_ranks = lax.axis_size("batch")
    table_ranks = lax.axis_size("table")
    user_count, seq_length, hash_count = item_rows.shape
    rows_local = tables.shape[1]
    model_width = tables.shape[2]
    per_rank = user_count // batch_ranks
    entry_count = user_count * seq_length * hash_count
    per_owner = entry_count // table_ranks
    leaving = item_rows[send_order].reshape(batch_ranks, per_rank, seq_length, hash_count)
    arrived = lax.all_to_all(leaving, "batch", split_axis=0, concat_axis=0, tiled=True).reshape(
        entry_count
    )
    owner_rank = arrived // rows_local
    hash_of = jnp.arange(entry_count, dtype=jnp.int32) % hash_count
    local_row = hash_of * rows_local + arrived % rows_local
    owner_onehot = (
        owner_rank[:, None] == jnp.arange(table_ranks, dtype=jnp.int32)[None, :]
    ).astype(jnp.int32)
    bucket_rank = jnp.sum((jnp.cumsum(owner_onehot, axis=0) - 1) * owner_onehot, axis=1)
    bucket_slot = owner_rank * per_owner + bucket_rank
    outgoing = (
        jnp.zeros((entry_count,), jnp.int32)
        .at[bucket_slot]
        .set(local_row)
        .reshape(table_ranks, per_owner)
    )
    token_of = (
        jnp.zeros((entry_count,), jnp.int32)
        .at[bucket_slot]
        .set(jnp.arange(entry_count, dtype=jnp.int32) // hash_count)
    )
    flat_table = tables.reshape(hash_count * rows_local, model_width)
    requested = lax.all_to_all(outgoing, "table", split_axis=0, concat_axis=0, tiled=True)
    served_rows = flat_table[requested]
    fetched = lax.all_to_all(served_rows, "table", split_axis=0, concat_axis=0, tiled=True)
    fetched_rows = fetched.reshape(entry_count, model_width)[bucket_slot]
    embedded = jnp.sum(
        fetched_rows.reshape(user_count * seq_length, hash_count, model_width).astype(jnp.float32),
        axis=1,
    )
    embedded = embedded.astype(jnp.bfloat16).reshape(user_count, seq_length, model_width)
    encoded, token_grad = run_layers(embedded, user_lengths, out_grad, w_in, w_out)
    token_grad = token_grad.reshape(user_count * seq_length, model_width)
    outgoing_grad = token_grad[token_of].reshape(table_ranks, per_owner, model_width)
    incoming = lax.all_to_all(outgoing_grad, "table", split_axis=0, concat_axis=0, tiled=True)
    dense_grad = jnp.zeros((hash_count * rows_local, model_width), jnp.float32)
    dense_grad = dense_grad.at[requested.reshape(-1)].add(incoming.reshape(-1, model_width))
    owned_grad = lax.psum_scatter(dense_grad, "batch", scatter_dimension=1, tiled=True)
    return (encoded, owned_grad.reshape(hash_count, rows_local, -1))


def solution(mesh):
    in_specs = (
        P(("batch", "table"), None, None),
        P(("batch", "table")),
        P(("batch", "table")),
        P(None, "table", None),
        P(),
        P(),
        P(("batch", "table"), None, None),
    )
    out_specs = (P(("batch", "table"), None, None), P(None, "table", "batch"))
    return jax.shard_map(body, mesh=mesh, in_specs=in_specs, out_specs=out_specs, check_vma=False)
```

profile of v0, /device:TPU:1, one launch (start us, length us, event | category | flops | bytes accessed | tf_op | source)
XLA Modules:
  0.0 468.0 jit_solution(7638861849887166186)
XLA Ops:
  10.6 11.2 %all_to_all.27 = s32[8,1,192]{2,1,0:T(1,128)S(1)} all-to-all(s32[8,1,192]{2,1,0:T(1,128)S(1)} %reshape.593), channel_id=1, replica_groups=mesh['batch'=8,'table'=16] {'batch'}, dimensions={0} | all-to-all | bytes 12288 | tf_op jit(solution)/shard_map/all_to_all | solution.py:86
  23.4 4.5 reduce-window.6
  28.8 6.2 %scatter_custom_fusion = s32[1536]{0:T(1024)S(1)} fusion(s32[1536]{0:T(1024)S(1)} %fusion.77, s32[1536]{0:T(1024)S(1)} %get-tuple-element.9, s32[]{:T(128)} %constant.70.clone.1), kind=kCustom, calls=%fused_computation.138 | custom fusion | bytes 6148 | tf_op jit(solution)/shard_map/scatter | solution.py:100
  35.1 13.0 %all_to_all.28 = s32[16,1,96]{2,1,0:T(1,128)S(1)} all-to-all(s32[16,1,96]{2,1,0:T(1,128)S(1)} %all_to_all.18), channel_id=1, replica_groups=mesh['batch'=8,'table'=16] {'table'}, dimensions={0} | all-to-all | bytes 12288 | tf_op jit(solution)/shard_map/all_to_all | solution.py:109
  48.1 11.4 %gather_fusion.1 = bf16[1536,1024]{1,0:T(8,128)(2,1)} fusion(bf16[3072,1024]{1,0:T(8,128)(2,1)} %bitcast.147, s32[2048]{0:T(1024)S(1)} %pad_clamp_fusion.2), kind=kCustom, calls=%fused_computation.1 | custom fusion | bytes 6297600 | tf_op jit(solution)/shard_map/gather | solution.py:110
  59.5 4.6 all-to-all-start.2
  67.8 6.6 %scatter_custom_fusion.1 = s32[1536]{0:T(1024)S(1)} fusion(s32[1536]{0:T(1024)S(1)} %fusion.77, s32[1536]{0:T(1024)S(1)} %add_select_fusion, s32[]{:T(128)} %constant.70.clone.1), kind=kCustom, calls=%fused_computation.140 | custom fusion | bytes 6148 | tf_op jit(solution)/shard_map/scatter | solution.py:106
  74.5 32.3 %all-to-all-done.2 = bf16[16,96,1024]{2,1,0:T(8,128)(2,1)} async-done(((bf16[16,96,1024]{2,1,0:T(8,128)(2,1)}), bf16[16,96,1024]{2,1,0:T(8,128)(2,1)}, u32[]{:S(2)}, u32[]{:S(2)}) %all-to-all-start.2) | async-done | bytes 3145760 | tf_op jit(solution)/shard_map/all_to_all | solution.py:111
  106.9 10.1 %gather_fusion.2 = bf16[1536,1024]{1,0:T(8,128)(2,1)} fusion(bf16[1536,1024]{1,0:T(8,128)(2,1)} %bitcast.5, s32[2048]{0:T(1024)S(1)} %pad_clamp_fusion.1), kind=kCustom, calls=%fused_computation.2 | custom fusion | bytes 6297600 | tf_op jit(solution)/shard_map/gather | solution.py:112
  117.0 9.1 %reshape.499 = bf16[512,3,1024]{2,1,0:T(4,128)(2,1)} reshape(bf16[1536,1024]{1,0:T(8,128)(2,1)} %gather_fusion.2) | data formatting | bytes 6291456 | tf_op jit(solution)/shard_map/reshape | solution.py:114
  126.1 7.3 %reduce_sum.115 = bf16[512,1024]{1,0:T(8,128)(2,1)S(1)} reduce(bf16[512,3,1024]{2,1,0:T(4,128)(2,1)} %reshape.499, bf16[]{:T(256)} %constant.81.clone.1), dimensions={1}, to_apply=%region_4.5 | reduce | flops 1048576 | bytes 4194306 | tf_op jit(solution)/shard_map/reduce_sum | solution.py:113
  134.0 11.7 %fusion.9 = (f32[512,4096]{1,0:T(8,128)}, f32[512,4096]{1,0:T(8,128)}) fusion(bf16[1,1024,4096]{2,1,0:T(8,128)(2,1)} %param.11, bf16[512,1024]{1,0:T(8,128)(2,1)S(1)} %reduce_sum.115, f32[512]{0:T(512)S(1)} %get-tuple-element.16, f32[512]{0:T(512)S(1)} %broadcast_multiply_fusion.1), kind=kOutput, calls=%fused_computation.18 | convolution fusion | flops 4305453056 | bytes 26218496 | tf_op jit(solution)/shard_map/jvp()/dot_general | solution.py:25
  145.8 10.9 %reshape.500 = f32[8,64,4,1024]{3,2,1,0:T(4,128)} reshape(f32[512,4096]{1,0:T(8,128)} %get-tuple-element.19) | data formatting | bytes 16777216 | tf_op jit(solution)/shard_map/jvp()/reshape | solution.py:26
  156.7 9.9 %copy.113 = bf16[8,64,4,1024]{3,1,0,2:T(8,128)(2,1)} copy(f32[8,64,4,1024]{3,2,1,0:T(4,128)} %reshape.500) | data formatting | bytes 12582912 | tf_op jit(solution)/shard_map/jvp()/reshape | solution.py:26
  166.6 4.9 %copy.60 = f32[8,64,4,1024]{3,1,0,2:T(8,128)S(1)} copy(f32[8,64,4,1024]{3,2,1,0:T(4,128)S(1)} %copy-done.1) | data formatting | bytes 16777216 | tf_op jit(solution)/shard_map/jvp()/reshape | solution.py:26
  171.5 4.5 fusion.89
  193.6 2.9 copy.74
  198.8 2.9 copy.76
  204.0 4.2 copy.64
  208.1 2.7 reshape.501
  210.8 2.7 fusion.28
  213.9 4.2 pad_add_fusion
  218.1 12.2 %copy.77 = f32[8,64,4,1024]{3,2,1,0:T(4,128)} copy(f32[8,64,4,1024]{3,1,0,2:T(8,128)} %pad_add_fusion) | data formatting | bytes 16777216 | tf_op jit(solution)/shard_map/transpose(jvp())/add_any | solution.py:27
  230.3 14.9 %copy.87 = f32[64,8,4,1024]{3,1,2,0:T(8,128)} copy(f32[64,8,4,1024]{3,2,1,0:T(4,128)} %bitcast.149) | data formatting | bytes 16777216
  245.2 12.9 %multiply_reduce_fusion = (f32[512]{0:T(512)S(1)}, f32[512,1024]{1,0:T(8,128)}) fusion(bf16[512,1024]{1,0:T(8,128)(2,1)S(1)} %reduce_sum.115, f32[512]{0:T(512)S(1)} %broadcast_multiply_fusion.1, bf16[1,1024,4096]{2,1,0:T(8,128)(2,1)} %param.11, f32[512,4096]{1,0:T(8,128)} %get-tuple-element.20, f32[512,4096]{1,0:T(8,128)} %bitcast.164), kind=kOutput, calls=%fused_computation.45 | convolution fusion | flops 4316986880 | bytes 28315648 | tf_op jit(solution)/shard_map/transpose(jvp())/dot_general | solution.py:25
  260.7 4.6 fusion.20
  265.2 9.4 %gather_fusion.3 = f32[1536,1024]{1,0:T(8,128)} fusion(f32[512,1024]{1,0:T(8,128)} %bitcast.146, s32[2048]{0:T(1024)S(1)} %pad_clamp_fusion), kind=kCustom, calls=%fused_computation.3 | custom fusion | bytes 12589056 | tf_op jit(solution)/shard_map/gather | solution.py:120
  274.6 5.0 %all-to-all-start.3 = ((f32[16,96,1024]{2,1,0:T(8,128)}), f32[16,96,1024]{2,1,0:T(8,128)}, u32[]{:S(2)}, u32[]{:S(2)}) async-start(f32[16,96,1024]{2,1,0:T(8,128)} %bitcast.151), calls=%async_computation.3 | async-start | bytes 12582912 | tf_op jit(solution)/shard_map/all_to_all | solution.py:121
  281.0 86.9 %all-to-all-done.3 = f32[16,96,1024]{2,1,0:T(8,128)} async-done(((f32[16,96,1024]{2,1,0:T(8,128)}), f32[16,96,1024]{2,1,0:T(8,128)}, u32[]{:S(2)}, u32[]{:S(2)}) %all-to-all-start.3) | async-done | bytes 6291488 | tf_op jit(solution)/shard_map/all_to_all | solution.py:121
  367.9 19.9 %scatter_custom_fusion.2 = f32[3072,1024]{1,0:T(8,128)} fusion(s32[1536]{0:T(1024)S(1)} %fusion.78, f32[1536,1024]{1,0:T(8,128)} %bitcast.23, f32[]{:T(128)} %constant.82.clone.1), kind=kCustom, calls=%fused_computation.19 | custom fusion | flops 1572864 | bytes 12583424 | tf_op jit(solution)/shard_map/scatter-add | solution.py:123
  387.8 5.1 %multiply_convert_fusion = bf16[8,64,1024]{2,1,0:T(8,128)(2,1)} fusion(f32[8,64,1024]{2,1,0:T(8,128)} %get-tuple-element.5, bf16[1,1024,1024]{2,1,0:T(8,128)(2,1)S(1)} %copy-done, f32[8,64,1,1024]{3,1,0,2:T(8,128)} %reshape.501, f32[8,64]{1,0:T(8,128)S(1)} %get-tuple-element.18, f32[8,64]{1,0:T(8,128)S(1)} %get-tuple-element.14, ...), kind=kOutput, calls=%fused_computation.48 | convolution fusion | flops 1077411840 | bytes 9443328 | tf_op jit(solution)/shard_map/jvp()/dot_general | solution.py:51
  393.0 68.0 %reduce-scatter.2.cloned.1.call-done = f32[3072,128]{1,0:T(8,128)} async-done(((f32[3072,1024]{1,0:T(8,128)}), f32[3072,128]{1,0:T(8,128)}) %reduce-scatter.2.cloned.1.call-update) | async-done | bytes 1572880 | tf_op jit(solution)/shard_map/reduce_scatter | solution.py:124
  (98 shorter events, 36.6 us)
Async XLA Ops:
  7.2 57.3 %copy-start = (bf16[1,1024,1024]{2,1,0:T(8,128)(2,1)S(1)}, bf16[1,1024,1024]{2,1,0:T(8,128)(2,1)}, u32[]{:S(2)}) copy-start(bf16[1,1024,1024]{2,1,0:T(8,128)(2,1)} %param.12) | copy-start | bytes 6291460
  59.5 4.6 copy-start.11
  59.5 4.7 %copy-start.7 = (bf16[8,64,1024]{2,1,0:T(8,128)(2,1)S(1)}, bf16[8,64,1024]{2,1,0:T(8,128)(2,1)}, u32[]{:S(2)}) copy-start(bf16[8,64,1024]{2,1,0:T(8,128)(2,1)} %param.13) | copy-start | bytes 3145732
  59.5 47.4 %all-to-all-start.2 = ((bf16[16,96,1024]{2,1,0:T(8,128)(2,1)}), bf16[16,96,1024]{2,1,0:T(8,128)(2,1)}, u32[]{:S(2)}, u32[]{:S(2)}) async-start(bf16[16,96,1024]{2,1,0:T(8,128)(2,1)} %bitcast.159), calls=%async_computation.2 | async-start | bytes 6291456 | tf_op jit(solution)/shard_map/all_to_all | solution.py:111
  65.8 1.9 copy-start.4
  156.7 9.9 %copy-start.1 = (f32[8,64,4,1024]{3,2,1,0:T(4,128)S(1)}, f32[8,64,4,1024]{3,2,1,0:T(4,128)}, u32[]{:S(2)}) copy-start(f32[8,64,4,1024]{3,2,1,0:T(4,128)} %reshape.500) | copy-start | bytes 25165828
  171.5 10.7 %copy-start.3 = (f32[8,64,4,1024]{3,1,0,2:T(8,128)}, f32[8,64,4,1024]{3,1,0,2:T(8,128)S(1)}, u32[]{:S(2)}) copy-start(f32[8,64,4,1024]{3,1,0,2:T(8,128)S(1)} %copy.60) | copy-start | bytes 25165828
  178.7 4.7 copy-start.2
  178.9 2.1 copy-start.6
  181.0 1.6 copy-start.5
  210.8 2.7 copy-start.8
  210.8 2.8 copy-start.9
  210.8 3.1 copy-start.10
  274.6 93.3 %all-to-all-start.3 = ((f32[16,96,1024]{2,1,0:T(8,128)}), f32[16,96,1024]{2,1,0:T(8,128)}, u32[]{:S(2)}, u32[]{:S(2)}) async-start(f32[16,96,1024]{2,1,0:T(8,128)} %bitcast.151), calls=%async_computation.3 | async-start | bytes 12582912 | tf_op jit(solution)/shard_map/all_to_all | solution.py:121
  279.7 181.2 %reduce-scatter.2.cloned.1.call-start = ((), (), s32[]{:S(2)}) async-start(), calls=%async_computation.5 | async-start | bytes 14155776 | tf_op jit(solution)/shard_map/reduce_scatter | solution.py:124
Sparse Core Ops, SparseCore 0:
  387.9 72.9 reduce-scatter.1
where the time goes:
time: 475 us; the launch traced here: 468 us
  waiting for transfers between devices  187 us (39%)
  local copies, waits for them, and re-layouts  142 us (30%)
  other arithmetic  52.7 us (11%)
  matrix products  38 us (8%)
  blocking collectives  24.2 us (5%)
  between operations  14.6 us (3%)
  starting transfers between devices  9.69 us (2%)
    all_to_all x1, waiting for transfers between devices, body(): lax.all_to_all(outgoing_grad, 'table', split_axis=0, concat_axis=0, tiled...  86.9 us
    reduce_scatter x1, waiting for transfers between devices, body(): lax.psum_scatter(dense_grad, 'batch', scatter_dimension=1, tiled=True)  68 us
    all_to_all x1, waiting for transfers between devices, body(): lax.all_to_all(served_rows, 'table', split_axis=0, concat_axis=0, tiled=T...  32.3 us
    reshape x3, local copies, waits for them, and re-layouts, hstu_block(): projected = projected.reshape(user_count, seq_length, 4, model_width)  25.7 us
    dot_general x2, matrix products, hstu_block(): jnp.dot(normed, w_in_layer, preferred_element_type=jnp.float32)  24.6 us
    unnamed x33, local copies, waits for them, and re-layouts  21.2 us
    scatter-add x1, other arithmetic, body(): dense_grad.at[requested.reshape(-1)].add(incoming.reshape(-1, model_width))  19.9 us
    all_to_all x1, blocking collectives, body(): lax.all_to_all(outgoing, 'table', split_axis=0, concat_axis=0, tiled=True)  13 us
  transfers between devices with their start and end apart: 3, of which 3 were waited for; matrix products, arithmetic and copies ran while one was open for 4% of the time, Pallas kernels for 0%

commit v1 on v0

v1 whole, which is shorter than its diff:
```python
import functools

import jax
import jax.numpy as jnp
from jax import lax
from jax.experimental import pallas as pl
from jax.experimental.pallas import tpu as pltpu
from jax.sharding import PartitionSpec as P

HEADS = 8
PER = 12
EPS = 1e-05
BF = jnp.bfloat16
F32 = jnp.float32
NT = (((1,), (1,)), ((), ()))
NN = (((1,), (0,)), ((), ()))
TN = (((0,), (0,)), ((), ()))
CHUNKS = 2
VMEM_LIMIT = 48 * 1024 * 1024


def dot(a, b, dims=NN):
    return lax.dot_general(a, b, dims, preferred_element_type=F32)


def iota(shape, dim):
    return lax.broadcasted_iota(jnp.int32, shape, dim)


def ids_kernel(order_ref, ids_ref, out_ref, ids_scr):
    users, owners = out_ref.shape[0], out_ref.shape[1]
    hashes, _, length = ids_ref.shape
    ids_scr[...] = jnp.full(ids_scr.shape, -1, jnp.int32)
    for b in range(users):
        user = order_ref[b]
        for h in range(hashes):
            ids_scr[b : b + 1, h * length : (h + 1) * length] = ids_ref[h, pl.ds(user, 1), :]
    ids = ids_scr[...]
    lanes = ids.shape[1]
    owner = lax.shift_right_arithmetic(ids, 10)
    hash_of = lax.div(iota(ids.shape, 1), length)
    code = (ids & 1023) + 1024 * hash_of
    high = (lax.shift_right_logical(code, 6)).astype(F32)
    low = (code & 63).astype(F32)
    hits = [jnp.where(owner == o, 1.0, 0.0).astype(F32) for o in range(owners)]
    before = jnp.where(iota((lanes, lanes), 0) < iota((lanes, lanes), 1), 1.0, 0.0).astype(BF)
    prefix = dot(jnp.concatenate(hits, axis=0).astype(BF), before)
    rank = jnp.zeros(ids.shape, F32)
    for o in range(owners):
        rank = rank + hits[o] * prefix[o * users : (o + 1) * users]
    rank = rank.astype(jnp.int32)
    total = jnp.zeros((2 * owners, 128), F32)
    for b in range(users):
        hit = iota((owners, lanes), 0) == owner[b : b + 1]
        left = jnp.concatenate(
            [jnp.where(hit, high[b : b + 1], 0.0), jnp.where(hit, low[b : b + 1], 0.0)], axis=0
        ).astype(BF)
        right = jnp.where(iota((128, lanes), 0) == rank[b : b + 1] + PER * b, 1.0, 0.0).astype(BF)
        total = total + dot(left, right, NT)
    codes = (total[:owners] * 64.0 + total[owners:]).astype(jnp.int32)
    slots = owner * 16 + rank
    for b in range(users):
        out_ref[b, :, :128] = codes
        out_ref[b, :, 128:] = jnp.broadcast_to(slots[b : b + 1], (owners, lanes))


def leaving_ids(order, ids, owners):
    users = ids.shape[1]
    return pl.pallas_call(
        ids_kernel,
        out_shape=jax.ShapeDtypeStruct((users, owners, 384), jnp.int32),
        in_specs=[
            pl.BlockSpec(memory_space=pltpu.SMEM),
            pl.BlockSpec(memory_space=pltpu.VMEM),
        ],
        out_specs=pl.BlockSpec(memory_space=pltpu.VMEM),
        scratch_shapes=[pltpu.VMEM((users, 256), jnp.int32)],
        compiler_params=pltpu.CompilerParams(vmem_limit_bytes=VMEM_LIMIT),
        name="leaving_ids",
    )(order, ids)


def serve_kernel(rank_ref, code_ref, table_hbm, *refs):
    outs = refs[:CHUNKS]
    raw, wide, stage, sems = refs[CHUNKS:]
    hashes, rows, width = table_hbm.shape
    tiles = width // 128
    copies = [
        pltpu.make_async_copy(table_hbm.at[h], raw.at[h], sems.at[h]) for h in range(hashes)
    ]
    for copy in copies:
        copy.start()
    for h in range(hashes):
        copies[h].wait()

        @pl.loop(0, rows // 16)
        def _(g):
            first = pl.multiple_of(g * 16, 16)
            for c in range(tiles):
                both = raw[h, pl.ds(first, 16), c * 128 : (c + 1) * 128].astype(F32)
                base = (h * rows + first) * tiles + c
                wide[pl.ds(base, 8, stride=tiles), :] = both[:8]
                wide[pl.ds(base + 8 * tiles, 8, stride=tiles), :] = both[8:]

    first_lane = rank_ref[0] * PER
    requesters, per_chunk, _ = outs[0].shape
    chunk_users = per_chunk // PER
    for chunk in range(CHUNKS):
        out_ref = outs[chunk]

        @pl.loop(0, requesters)
        def _(t):
            for j in range(chunk_users):
                home = (chunk * chunk_users + j) * requesters + t
                for k in range(PER):
                    row = code_ref[home, first_lane + k]
                    slot = (j * PER + k) * tiles
                    stage[slot : slot + tiles, :] = wide[
                        pl.ds(pl.multiple_of(row * tiles, tiles), tiles), :
                    ]
            for g in range(per_chunk // 16):
                for c in range(tiles):
                    base = g * 16 * tiles + c
                    upper = stage[pl.ds(base, 8, stride=tiles), :]
                    lower = stage[pl.ds(base + 8 * tiles, 8, stride=tiles), :]
                    out_ref[t, g * 16 : (g + 1) * 16, c * 128 : (c + 1) * 128] = jnp.concatenate(
                        [upper, lower], axis=0
                    ).astype(BF)


def serve_rows(rank, got, tables, requesters, per_chunk):
    hashes, rows, width = tables.shape
    tiles = width // 128
    return pl.pallas_call(
        serve_kernel,
        out_shape=[jax.ShapeDtypeStruct((requesters, per_chunk, width), BF)] * CHUNKS,
        grid=(1,),
        in_specs=[
            pl.BlockSpec(memory_space=pltpu.SMEM),
            pl.BlockSpec((got.shape[0], 128), lambda i: (0, 0), memory_space=pltpu.SMEM),
            pl.BlockSpec(memory_space=pl.ANY),
        ],
        out_specs=[pl.BlockSpec((requesters, per_chunk, width), lambda i: (0, 0, 0))] * CHUNKS,
        scratch_shapes=[
            pltpu.VMEM((hashes, rows, width), BF),
            pltpu.VMEM((hashes * rows * tiles, 128), F32),
            pltpu.VMEM((per_chunk * tiles, 128), F32),
            pltpu.SemaphoreType.DMA((hashes,)),
        ],
        compiler_params=pltpu.CompilerParams(vmem_limit_bytes=VMEM_LIMIT),
        name="serve_rows",
    )(rank, got, tables)


def sigmoid(z):
    return 0.5 + 0.5 * jnp.tanh(0.5 * z)


def layer_kernel(
    chunk, len_ref, slot_ref, fetched_ref, cot_ref, w_in_hbm, w_out_hbm, enc_ref, grad_ref,
    win, wout, x_s, n_s, gate_s, dsilu_s, qkv_s, mixed_s, w_s, dw_s, dz_s, live_s, sems,
):
    users, length, width = cot_ref.shape
    tokens = users * length
    head = width // HEADS
    owners, per_chunk, _ = fetched_ref.shape
    slots = owners * per_chunk
    pair = 2 * length
    pairs = tokens // pair
    copies = [
        pltpu.make_async_copy(
            w_in_hbm.at[0, :, pl.ds(c * width, width)], win.at[c], sems.at[c]
        )
        for c in range(4)
    ] + [pltpu.make_async_copy(w_out_hbm.at[0], wout, sems.at[4])]
    for copy in copies:
        copy.start()

    slot_rows = []
    for h in range(3):
        packed = slot_ref[h : h + 1, :]
        slot_rows.append(
            lax.shift_right_logical(packed, 4) * per_chunk
            + lax.div(iota((1, tokens), 1), length) * PER
            + (packed & 15)
        )
    stacked = jnp.concatenate(slot_rows + [jnp.zeros((5, tokens), jnp.int32)], axis=0)
    slot_cols = stacked.astype(F32).T.astype(jnp.int32)
    lane = iota((tokens, slots), 1)
    pick = (
        (lane == slot_cols[:, 0:1]) | (lane == slot_cols[:, 1:2]) | (lane == slot_cols[:, 2:3])
    )
    pick = jnp.where(pick, 1.0, 0.0).astype(BF)
    x = dot(pick, fetched_ref[...].reshape(slots, width)).astype(BF).astype(F32)
    x_s[...] = x
    mean = jnp.mean(x, axis=1, keepdims=True)
    centered = x - mean
    rstd = lax.rsqrt(jnp.mean(centered * centered, axis=1, keepdims=True) + EPS)
    n_s[...] = (centered * rstd).astype(BF)

    token_user = lax.div(iota((tokens, 1), 0), length)
    token_pos = iota((tokens, 1), 0) - token_user * length
    token_len = jnp.zeros((tokens, 1), jnp.int32)
    for u in range(users):
        token_len = jnp.where(token_user == u, len_ref[chunk * users + u], token_len)
    live = jnp.where(token_pos < token_len, 1.0, 0.0).astype(F32)
    key = iota((tokens, pair), 1)
    query = iota((tokens, pair), 0)
    same = lax.div(key, length) == lax.rem(lax.div(query, length), 2)
    causal = lax.rem(key, length) <= lax.rem(query, length)
    live_s[...] = jnp.where(same & causal, 1.0, 0.0) * live

    step = 256
    for c in range(4):
        copies[c].wait()

        @pl.loop(0, width // step)
        def _(i):
            cols = pl.ds(pl.multiple_of(i * step, step), step)
            z = dot(n_s[...], win[c, :, cols])
            sig = sigmoid(z)
            out = z * sig
            dsilu_s[c, :, cols] = sig + out * (1.0 - sig)
            if c == 0:
                gate_s[:, cols] = out
            else:
                qkv_s[c - 1, :, cols] = out.astype(BF)

    scale = head ** (-0.5)
    for p in range(pairs):
        rows = slice(p * pair, (p + 1) * pair)
        for h in range(HEADS):
            cols = slice(h * head, (h + 1) * head)
            s = dot(qkv_s[1, rows, cols], qkv_s[2, rows, cols], NT) * scale
            mask = live_s[rows, :]
            sig = sigmoid(s)
            out = s * sig
            w = (out * mask).astype(BF)
            w_s[p * HEADS + h] = w
            dw_s[p * HEADS + h] = (sig + out * (1.0 - sig)) * (mask * scale)
            mixed_s[rows, cols] = dot(w, qkv_s[0, rows, cols])

    mixed = mixed_s[...]
    mean2 = jnp.mean(mixed, axis=1, keepdims=True)
    centered2 = mixed - mean2
    rstd2 = lax.rsqrt(jnp.mean(centered2 * centered2, axis=1, keepdims=True) + EPS)
    hat = centered2 * rstd2
    gate = gate_s[...]
    gated = (hat * gate).astype(BF)
    copies[4].wait()
    out = (x_s[...] + dot(gated, wout[...])) * live
    enc_ref[...] = out.astype(BF).reshape(users, length, width)

    g = cot_ref[...].reshape(tokens, width).astype(F32) * live
    dgated = dot(g.astype(BF), wout[...], NT).astype(BF).astype(F32)
    dz_s[0] = (dgated * hat * dsilu_s[0]).astype(BF)
    dhat = dgated * gate
    dmixed = rstd2 * (
        dhat
        - jnp.mean(dhat, axis=1, keepdims=True)
        - hat * jnp.mean(dhat * hat, axis=1, keepdims=True)
    )
    n_mixed = dmixed.astype(BF)
    for p in range(pairs):
        rows = slice(p * pair, (p + 1) * pair)
        for h in range(HEADS):
            cols = slice(h * head, (h + 1) * head)
            dm = n_mixed[rows, cols]
            v, q, k = (qkv_s[i, rows, cols] for i in range(3))
            dweights = dot(dm, v, NT).astype(BF).astype(F32)
            ds = (dweights * dw_s[p * HEADS + h]).astype(BF)
            dv = dot(w_s[p * HEADS + h], dm, TN).astype(BF).astype(F32)
            dq = dot(ds, k).astype(BF).astype(F32)
            dk = dot(ds, q, TN).astype(BF).astype(F32)
            dz_s[1, rows, cols] = (dv * dsilu_s[1, rows, cols]).astype(BF)
            dz_s[2, rows, cols] = (dq * dsilu_s[2, rows, cols]).astype(BF)
            dz_s[3, rows, cols] = (dk * dsilu_s[3, rows, cols]).astype(BF)

    @pl.loop(0, width // step)
    def _(i):
        cols = pl.ds(pl.multiple_of(i * step, step), step)
        dn = dot(dz_s[0], win[0, cols, :], NT)
        for c in range(1, 4):
            dn = dn + dot(dz_s[c], win[c, cols, :], NT)
        mixed_s[:, cols] = dn

    dn = mixed_s[...].astype(BF).astype(F32)
    x = x_s[...]
    xhat = (x - mean) * rstd
    dx = rstd * (
        dn
        - jnp.mean(dn, axis=1, keepdims=True)
        - xhat * jnp.mean(dn * xhat, axis=1, keepdims=True)
    )
    token_grad = (dx + g).astype(BF)
    n_s[...] = token_grad
    for t in range(owners):
        sub = iota((per_chunk, tokens), 0) + t * per_chunk
        put = (sub == slot_rows[0]) | (sub == slot_rows[1]) | (sub == slot_rows[2])
        rows_out = dot(jnp.where(put, 1.0, 0.0).astype(BF), n_s[...]).astype(BF)
        for b in range(grad_ref.shape[0]):
            grad_ref[b, t] = rows_out[:, b * 128 : (b + 1) * 128]


def layer(chunk, lengths, slots, fetched, cot, w_in, w_out, batch_ranks):
    owners, per_chunk, width = fetched.shape
    users, length, _ = cot.shape
    users //= CHUNKS
    tokens = users * length
    blocks = (users // 2) * HEADS
    return pl.pallas_call(
        functools.partial(layer_kernel, chunk),
        out_shape=[
            jax.ShapeDtypeStruct((users, length, width), BF),
            jax.ShapeDtypeStruct((batch_ranks, owners, per_chunk, width // batch_ranks), BF),
        ],
        grid=(1,),
        in_specs=[
            pl.BlockSpec(memory_space=pltpu.SMEM),
            pl.BlockSpec((3, tokens), lambda i: (0, 0)),
            pl.BlockSpec((owners, per_chunk, width), lambda i: (0, 0, 0)),
            pl.BlockSpec((users, length, width), lambda i: (chunk, 0, 0)),
            pl.BlockSpec(memory_space=pl.ANY),
            pl.BlockSpec(memory_space=pl.ANY),
        ],
        out_specs=[
            pl.BlockSpec((users, length, width), lambda i: (0, 0, 0)),
            pl.BlockSpec(
                (batch_ranks, owners, per_chunk, width // batch_ranks), lambda i: (0, 0, 0, 0)
            ),
        ],
        scratch_shapes=[
            pltpu.VMEM((4, width, width), BF),
            pltpu.VMEM((width, width), BF),
            pltpu.VMEM((tokens, width), F32),
            pltpu.VMEM((tokens, width), BF),
            pltpu.VMEM((tokens, width), F32),
            pltpu.VMEM((4, tokens, width), F32),
            pltpu.VMEM((3, tokens, width), BF),
            pltpu.VMEM((tokens, width), F32),
            pltpu.VMEM((blocks, 2 * length, 2 * length), BF),
            pltpu.VMEM((blocks, 2 * length, 2 * length), F32),
            pltpu.VMEM((4, tokens, width), BF),
            pltpu.VMEM((tokens, 2 * length), F32),
            pltpu.SemaphoreType.DMA((5,)),
        ],
        compiler_params=pltpu.CompilerParams(vmem_limit_bytes=VMEM_LIMIT),
        cost_estimate=pl.CostEstimate(
            flops=12_000_000_000 // CHUNKS, bytes_accessed=16_000_000, transcendentals=2_000_000
        ),
        name="layer",
    )(lengths, slots, fetched, cot, w_in, w_out)


def collect_kernel(first, *refs):
    if first:
        code_ref, rows_ref, out_ref = refs
    else:
        code_ref, rows_ref, prev_ref, out_ref = refs
    steps, depth = code_ref.shape
    tile = 512

    @pl.loop(0, out_ref.shape[0] // tile)
    def _(m):
        start = pl.multiple_of(m * tile, tile)
        acc = jnp.zeros((tile, 128), F32) if first else prev_ref[pl.ds(start, tile), :]
        for s in range(steps):
            hit = iota((tile, depth), 0) == code_ref[s : s + 1, :] - start
            acc = acc + dot(
                jnp.where(hit, 1.0, 0.0).astype(BF), rows_ref[s * depth : (s + 1) * depth, :]
            )
        out_ref[pl.ds(start, tile), :] = acc


def collect(codes, rows, prev, total):
    first = prev is None
    args = (codes, rows) if first else (codes, rows, prev)
    return pl.pallas_call(
        functools.partial(collect_kernel, first),
        out_shape=jax.ShapeDtypeStruct((total, 128), F32),
        in_specs=[pl.BlockSpec(memory_space=pltpu.VMEM)] * len(args),
        out_specs=pl.BlockSpec(memory_space=pltpu.VMEM),
        compiler_params=pltpu.CompilerParams(vmem_limit_bytes=VMEM_LIMIT),
        cost_estimate=pl.CostEstimate(
            flops=10_000_000_000 // CHUNKS, bytes_accessed=6_000_000, transcendentals=0
        ),
        name="collect",
    )(*args)


def body(item_rows, send_order, user_lengths, tables, w_in, w_out, out_grad):
    batch_ranks = lax.axis_size("batch")
    table_ranks = lax.axis_size("table")
    users, length, hashes = item_rows.shape
    rows_local = tables.shape[1]
    both = ("batch", "table")
    chunk_users = users // CHUNKS
    per_chunk = chunk_users * PER

    leaving = leaving_ids(send_order, item_rows.transpose(2, 0, 1), table_ranks)
    got = lax.all_to_all(
        leaving.reshape(batch_ranks * table_ranks, 384), both, 0, 0, tiled=True
    )
    homes = got.reshape(users, table_ranks, 384)
    rank = lax.axis_index("batch").astype(jnp.int32)[None]
    served = serve_rows(rank, got, tables, table_ranks, per_chunk)

    mine = lax.dynamic_index_in_dim(homes, lax.axis_index("table"), 1, keepdims=False)
    slots = mine[:, 128 : 128 + hashes * length].reshape(users, hashes, length)
    slots = slots.transpose(1, 0, 2)
    codes = homes[:, :, : batch_ranks * PER].reshape(users, table_ranks, batch_ranks, PER)
    codes = codes.transpose(2, 1, 0, 3)

    encoded, total = [], None
    returned = []
    for c in range(CHUNKS):
        part = slice(c * chunk_users, (c + 1) * chunk_users)
        fetched = lax.all_to_all(served[c], "table", 0, 0, tiled=True)
        enc, grads = layer(
            c, user_lengths, slots[:, part].reshape(hashes, chunk_users * length), fetched,
            out_grad, w_in, w_out, batch_ranks,
        )
        encoded.append(enc)
        grads = grads.reshape(batch_ranks * table_ranks, per_chunk, -1)
        returned.append(lax.all_to_all(grads, both, 0, 0, tiled=True))
    for c in range(CHUNKS):
        part = slice(c * chunk_users, (c + 1) * chunk_users)
        rows = returned[c].reshape(batch_ranks * table_ranks * per_chunk, -1)
        total = collect(
            codes[:, :, part].reshape(-1, 512), rows, total, hashes * rows_local
        )
    return jnp.concatenate(encoded, axis=0), total.reshape(hashes, rows_local, -1)


def solution(mesh):
    in_specs = (
        P(("batch", "table"), None, None),
        P(("batch", "table")),
        P(("batch", "table")),
        P(None, "table", None),
        P(),
        P(),
        P(("batch", "table"), None, None),
    )
    out_specs = (P(("batch", "table"), None, None), P(None, "table", "batch"))
    return jax.shard_map(body, mesh=mesh, in_specs=in_specs, out_specs=out_specs, check_vma=False)
```

time: 475 us -> 171 us (0.36); the launches traced: 468 us -> 170 us
  waiting for transfers between devices: 187 us -> 12.9 us
  local copies, waits for them, and re-layouts: 142 us -> 19.3 us
  Pallas kernels: 0 us -> 76.4 us
  other arithmetic: 52.7 us -> 2.26 us
  matrix products: 38 us -> 0 us
  starting transfers between devices: 9.69 us -> 34.2 us
  between operations: 14.6 us -> 0.82 us
    all_to_all x2 -> x4, waiting for transfers between devices: 119 us -> 12.9 us  [the longest x1 10.6 us: body(): lax.all_to_all(leaving.reshape(batch_ranks * table_ranks, 384), both, 0,...]
    pallas_call x0 -> x6, Pallas kernels: none -> 76.4 us  [the longest x2 41.2 us: layer(): pl.pallas_call(functools.partial(layer_kernel, chunk), out_shape=[jax.Sha...]
    reduce_scatter x1 -> x0, waiting for transfers between devices: 68 us -> none  [body(): lax.psum_scatter(dense_grad, 'batch', scatter_dimension=1, tiled=True)]
    dot_general x10 -> x0, matrix products: 38 us -> none  [the longest x2 24.6 us: hstu_block(): jnp.dot(normed, w_in_layer, preferred_element_type=jnp.float32)]
    reshape x10 -> x6, local copies, waits for them, and re-layouts: 38.2 us -> 3.64 us  [the longest x2 2.41 us: body(): codes[:, :, part].reshape(-1, 512)]
    gather x4 -> x0, local copies, waits for them, and re-layouts: 32.1 us -> none  [the longest x1 11.4 us: body(): served_rows = flat_table[requested]]
    all_to_all x2 -> x4, starting transfers between devices: 9.65 us -> 34.2 us  [the longest x2 18.8 us: body(): returned.append(lax.all_to_all(grads, both, 0, 0, tiled=True))]
    scatter-add x1 -> x0, other arithmetic: 19.9 us -> none  [body(): dense_grad.at[requested.reshape(-1)].add(incoming.reshape(-1, model_width))]
  transfers between devices with their start and end apart: 3 -> 4, of which waited for: 3 -> 3; matrix products, arithmetic and copies ran while one was open for 4% -> 6% of each run, Pallas kernels for 0% -> 30%
where the time goes in v1:
time: 171 us; the launch traced here: 170 us
  Pallas kernels  76.4 us (45%)
  starting transfers between devices  34.2 us (20%)
  blocking collectives  24.4 us (14%)
  local copies, waits for them, and re-layouts  19.3 us (11%)
  waiting for transfers between devices  12.9 us (8%)
  other arithmetic  2.26 us (1%)
    pallas_call x2, Pallas kernels, layer(): pl.pallas_call(functools.partial(layer_kernel, chunk), out_shape=[jax.Sha...  41.2 us
    all_to_all x1, blocking collectives, body(): fetched = lax.all_to_all(served[c], 'table', 0, 0, tiled=True)  24.4 us
    pallas_call x2, Pallas kernels, collect(): pl.pallas_call(functools.partial(collect_kernel, first), out_shape=jax.Sh...  22.6 us
    all_to_all x2, starting transfers between devices, body(): returned.append(lax.all_to_all(grads, both, 0, 0, tiled=True))  18.8 us
    pallas_call x1, Pallas kernels, serve_rows(): pl.pallas_call(serve_kernel, out_shape=[jax.ShapeDtypeStruct((requesters,...  11.6 us
    all_to_all x1, starting transfers between devices, body(): lax.all_to_all(leaving.reshape(batch_ranks * table_ranks, 384), both, 0,...  11.5 us
    all_to_all x1, waiting for transfers between devices, body(): lax.all_to_all(leaving.reshape(batch_ranks * table_ranks, 384), both, 0,...  10.6 us
    unnamed x24, local copies, waits for them, and re-layouts  10.3 us
  transfers between devices with their start and end apart: 4, of which 3 were waited for; matrix products, arithmetic and copies ran while one was open for 6% of the time, Pallas kernels for 30%

profile of v1, /device:TPU:1, one launch (start us, length us, event | category | flops | bytes accessed | tf_op | source)
XLA Modules:
  0.0 170.2 jit_solution(5419815105109394666)
XLA Ops:
  0.6 0.7 copy-done.4
  1.3 0.7 copy-done.5
  2.0 1.1 leaving_ids.1
  3.1 0.9 copy.13
  4.0 11.5 %all-to-all-start = ((s32[128,1,384]{2,1,0:T(1,128)}), s32[128,1,384]{2,1,0:T(1,128)S(1)}, u32[]{:S(2)}, u32[]{:S(2)}) async-start(s32[128,1,384]{2,1,0:T(1,128)} %copy.13), calls=%async_computation | async-start | bytes 393216 | tf_op jit(solution)/shard_map/all_to_all | solution.py:401
  15.5 10.6 %all-to-all-done = s32[128,1,384]{2,1,0:T(1,128)S(1)} async-done(((s32[128,1,384]{2,1,0:T(1,128)}), s32[128,1,384]{2,1,0:T(1,128)S(1)}, u32[]{:S(2)}, u32[]{:S(2)}) %all-to-all-start) | async-done | bytes 196640 | tf_op jit(solution)/shard_map/all_to_all | solution.py:401
  26.1 11.6 %serve_rows.1 = (bf16[16,48,1024]{2,1,0:T(8,128)(2,1)S(1)}, bf16[16,48,1024]{2,1,0:T(8,128)(2,1)}) custom-call(s32[1]{0:T(128)} %bitcast.3.rank_ref, s32[128,384]{1,0:T(8,128)S(1)} %bitcast.21, bf16[3,1024,1024]{2,1,0:T(8,128)(2,1)} %table_hbm.1), custom_call_target="tpu_custom_call" | custom-call | tf_op jit(solution)/shard_map/serve_rows/pallas_call | solution.py:134
  37.7 24.4 %all_to_all.31.fetched_ref = bf16[16,48,1024]{2,1,0:T(8,128)(2,1)S(1)} all-to-all(bf16[16,48,1024]{2,1,0:T(8,128)(2,1)S(1)} %get-tuple-element.8), channel_id=1, replica_groups=mesh['batch'=8,'table'=16] {'table'}, dimensions={0} | all-to-all | bytes 3145728 | tf_op jit(solution)/shard_map/all_to_all | solution.py:418
  62.0 3.8 %all-to-all-start.2 = ((bf16[16,48,1024]{2,1,0:T(8,128)(2,1)}), bf16[16,48,1024]{2,1,0:T(8,128)(2,1)S(1)}, u32[]{:S(2)}, u32[]{:S(2)}) async-start(bf16[16,48,1024]{2,1,0:T(8,128)(2,1)} %get-tuple-element.10), calls=%async_computation.2 | async-start | bytes 3145728 | tf_op jit(solution)/shard_map/all_to_all | solution.py:418
  66.1 1.2 copy-done.6
  67.3 20.6 %layer.2 = (bf16[4,64,1024]{2,1,0:T(8,128)(2,1)S(1)}, bf16[8,16,48,128]{3,2,1,0:T(8,128)(2,1)S(1)}) custom-call(s32[8]{0:T(128)S(1)} %copy-done.8, s32[3,256]{1,0:T(4,128)S(1)} %reshape.47.slot_ref, bf16[16,48,1024]{2,1,0:T(8,128)(2,1)S(1)} %all_to_all.31.fetched_ref, bf16[8,64,1024]{2,1,0:T(8,128)(2,1)S(1)} %copy-done.6, bf16[1,1024,4096]{2,1,0:T(8,128)(2,1)} %w_in_hbm.3, ...), custom_call_target="tpu_custom_call" | custom-call | flops 6000000000 | bytes 16000000 | tf_op jit(solution)/shard_map/layer/pallas_call | solution.py:311
  87.9 1.2 copy-done.1
  89.1 0.8 copy-done.2
  89.9 9.3 %all-to-all-start.4 = ((bf16[128,48,128]{2,1,0:T(8,128)(2,1)}), bf16[128,48,128]{2,1,0:T(8,128)(2,1)S(1)}, u32[]{:S(2)}, u32[]{:S(2)}) async-start(bf16[128,48,128]{2,1,0:T(8,128)(2,1)} %bitcast.20), calls=%async_computation.4 | async-start | bytes 3145728 | tf_op jit(solution)/shard_map/all_to_all | solution.py:425
  99.2 1.2 copy-done.7
  100.5 20.6 %layer.3 = (bf16[4,64,1024]{2,1,0:T(8,128)(2,1)S(1)}, bf16[8,16,48,128]{3,2,1,0:T(8,128)(2,1)S(1)}) custom-call(s32[8]{0:T(128)S(1)} %copy-done.8, s32[3,256]{1,0:T(4,128)S(1)} %reshape.48.slot_ref, bf16[16,48,1024]{2,1,0:T(8,128)(2,1)S(1)} %all-to-all-done.2.fetched_ref, bf16[8,64,1024]{2,1,0:T(8,128)(2,1)S(1)} %copy-done.7, ...), custom_call_target="tpu_custom_call" | custom-call | flops 6000000000 | bytes 16000000 | tf_op jit(solution)/shard_map/layer/pallas_call | solution.py:311
  121.1 1.1 copy-done
  122.2 0.8 copy-done.3
  123.0 0.2 all-to-all-done.4
  123.2 9.5 %all-to-all-start.3 = ((bf16[128,48,128]{2,1,0:T(8,128)(2,1)}), bf16[128,48,128]{2,1,0:T(8,128)(2,1)S(1)}, u32[]{:S(2)}, u32[]{:S(2)}) async-start(bf16[128,48,128]{2,1,0:T(8,128)(2,1)} %bitcast.18), calls=%async_computation.3 | async-start | bytes 3145728 | tf_op jit(solution)/shard_map/all_to_all | solution.py:425
  132.8 1.0 reshape.49
  133.8 1.8 %fusion = (s32[8,16,4,12]{3,0,1,2:T(8,128)S(1)}, s32[8,16,4,12]{3,0,1,2:T(8,128)}) fusion(s32[8,16,8,12]{3,0,1,2:T(8,128)} %bitcast.26), kind=kLoop, calls=%fused_computation.4 | loop fusion | bytes 98304 | tf_op jit(solution)/shard_map/slice | solution.py:430
  135.5 0.9 copy.17
  136.4 1.2 reshape.53.refs_0_
  137.6 1.8 %copy.16 = s32[8,16,4,12]{3,2,1,0:T(4,128)} copy(s32[8,16,4,12]{3,0,1,2:T(8,128)} %get-tuple-element.15) | data formatting | bytes 49152 | tf_op jit(solution)/shard_map/slice | solution.py:430
  139.5 1.2 reshape.50.refs_0_
  140.7 2.3 %pad_maximum_fusion = bf16[8,64,1024]{2,1,0:T(8,128)(2,1)} fusion(bf16[4,64,1024]{2,1,0:T(8,128)(2,1)} %copy-done.3, bf16[4,64,1024]{2,1,0:T(8,128)(2,1)} %copy-done.2), kind=kLoop, calls=%fused_computation | loop fusion | flops 524288 | bytes 2097152 | tf_op jit(solution)/shard_map/concatenate | solution.py:432
  142.9 10.7 %collect.2.refs_2_ = f32[3072,128]{1,0:T(8,128)S(1)} custom-call(s32[12,512]{1,0:T(8,128)S(1)} %reshape.53.refs_0_, bf16[6144,128]{1,0:T(8,128)(2,1)S(1)} %bitcast.17), custom_call_target="tpu_custom_call" | custom-call | flops 5000000000 | bytes 6000000 | tf_op jit(solution)/shard_map/collect/pallas_call | solution.py:378
  153.7 1.2 copy-done.9
  154.8 2.1 %all-to-all-done.3 = bf16[128,48,128]{2,1,0:T(8,128)(2,1)S(1)} async-done(((bf16[128,48,128]{2,1,0:T(8,128)(2,1)}), bf16[128,48,128]{2,1,0:T(8,128)(2,1)S(1)}, u32[]{:S(2)}, u32[]{:S(2)}) %all-to-all-start.3) | async-done | bytes 1572896 | tf_op jit(solution)/shard_map/all_to_all | solution.py:425
  156.9 1.4 copy-done.10
  158.3 11.9 %collect.3 = f32[3072,128]{1,0:T(8,128)} custom-call(s32[12,512]{1,0:T(8,128)S(1)} %reshape.50.refs_0_, bf16[6144,128]{1,0:T(8,128)(2,1)S(1)} %bitcast.19, f32[3072,128]{1,0:T(8,128)S(1)} %copy-done.10), custom_call_target="tpu_custom_call" | custom-call | flops 5000000000 | bytes 6000000 | tf_op jit(solution)/shard_map/collect/pallas_call | solution.py:378
  (24 shorter events, 0.3 us)
Async XLA Ops:
  0.6 0.7 copy-start.4
  1.3 0.7 copy-start.5
  4.0 22.1 %all-to-all-start = ((s32[128,1,384]{2,1,0:T(1,128)}), s32[128,1,384]{2,1,0:T(1,128)S(1)}, u32[]{:S(2)}, u32[]{:S(2)}) async-start(s32[128,1,384]{2,1,0:T(1,128)} %copy.13), calls=%async_computation | async-start | bytes 393216 | tf_op jit(solution)/shard_map/all_to_all | solution.py:401
  62.0 4.1 %copy-start.8 = (s32[8]{0:T(128)S(1)}, s32[8]{0:T(128)}, u32[]{:S(2)}) copy-start(s32[8]{0:T(128)} %len_ref.3) | copy-start | bytes 100
  62.0 27.8 %all-to-all-start.2 = ((bf16[16,48,1024]{2,1,0:T(8,128)(2,1)}), bf16[16,48,1024]{2,1,0:T(8,128)(2,1)S(1)}, u32[]{:S(2)}, u32[]{:S(2)}) async-start(bf16[16,48,1024]{2,1,0:T(8,128)(2,1)} %get-tuple-element.10), calls=%async_computation.2 | async-start | bytes 3145728 | tf_op jit(solution)/shard_map/all_to_all | solution.py:418
  66.1 1.2 copy-start.6
  87.9 1.2 copy-start.1
  89.1 0.8 copy-start.2
  89.9 33.4 %all-to-all-start.4 = ((bf16[128,48,128]{2,1,0:T(8,128)(2,1)}), bf16[128,48,128]{2,1,0:T(8,128)(2,1)S(1)}, u32[]{:S(2)}, u32[]{:S(2)}) async-start(bf16[128,48,128]{2,1,0:T(8,128)(2,1)} %bitcast.20), calls=%async_computation.4 | async-start | bytes 3145728 | tf_op jit(solution)/shard_map/all_to_all | solution.py:425
  99.2 1.2 copy-start.7
  121.1 1.1 copy-start
  122.2 0.8 copy-start.3
  123.2 33.6 %all-to-all-start.3 = ((bf16[128,48,128]{2,1,0:T(8,128)(2,1)}), bf16[128,48,128]{2,1,0:T(8,128)(2,1)S(1)}, u32[]{:S(2)}, u32[]{:S(2)}) async-start(bf16[128,48,128]{2,1,0:T(8,128)(2,1)} %bitcast.18), calls=%async_computation.3 | async-start | bytes 3145728 | tf_op jit(solution)/shard_map/all_to_all | solution.py:425
  153.7 1.2 copy-start.9
  156.9 1.4 copy-start.10
